TPU v7x, 32 devices: a whole 2x2x4 slice. The times are simulated.
32 devices in a mesh: groups: 2 (over x), tm: 16 (over z, y, core).
Axes of the slice: x: 2, y: 2, z: 4, core: 2. Of those that a mesh axis runs over, the one named last changes fastest.
Arguments:
- gauge_series: bfloat16 [2048, 8192], P('groups', 'tm'), parts along dimension 0, may hold values from -6 to 6
- gauge_order: int32 [8192], replicated, may hold values from 0 to 8191, each once
- gauge_block: int32 [8192], replicated, may hold values from 0 to 3
- gauge_weight: bfloat16 [8192, 64], replicated, may hold values from -0.125 to 0.125
- filt_trans: float32 [512, 256], P('groups'), parts along dimension 0, may hold values from -2 to 2
- obs_gain: float32 [512, 256], P('groups'), parts along dimension 0, may hold values from -2 to 2
- smooth_gain: float32 [512, 256], P('groups'), parts along dimension 0, may hold values from -2 to 2
Outputs:
- filtered_mean: float32 [2048, 256], P(('groups', 'tm')), parts along dimension 0
- smoothed_mean: float32 [2048, 256], P(('groups', 'tm')), parts along dimension 0
There are 2 independent parts, one for each index of `groups`. A program takes and returns all parts, laid end to end along the dimension named above; an argument that names none is the same for every part. Nothing has to cross between parts.
Inputs may be any that keep to these rules, and one draw needn't show every extreme that they name: `gauge_order`: each gauge appears in exactly one column.
All inputs are finite; a program needn't handle non-finite values.
Results may differ from a plain program's by a relative error of at most 0.0003.
Values may be sent and summed in bfloat16 or wider, within the bound.
A program may use at most 128 MiB of HBM per device.

v0:
```python
import jax
import jax.numpy as jnp
from jax import lax
from jax.sharding import PartitionSpec as P

PRECISE = lax.Precision.HIGHEST


def carried_in(array, axis, combine, identity, reverse):
    size, place = (lax.axis_size(axis), lax.axis_index(axis))
    everything = jax.tree.map(lambda part: lax.all_gather(part, axis), array)
    start = jax.tree.map(
        lambda part, zero: jnp.broadcast_to(jnp.asarray(zero, part.dtype), part.shape),
        array,
        identity,
    )

    def hop(k, before):
        at = size - 1 - k if reverse else k
        reached = at > place if reverse else at < place
        new = combine(before, jax.tree.map(lambda part: part[at], everything))
        return jax.tree.map(lambda a, b: jnp.where(reached, a, b), new, before)

    return lax.fori_loop(0, size, hop, start)


def matmul(left, right):
    return jnp.dot(left, right, precision=PRECISE, preferred_element_type=jnp.float32)


def apply_rows(values, matrix):
    return lax.dot_general(
        values,
        matrix,
        (((1,), (1,)), ((), ())),
        precision=PRECISE,
        preferred_element_type=jnp.float32,
    )


def square_table(matrix, tree_depth):
    powers = [matrix]
    for height in range(tree_depth):
        powers.append(matmul(powers[-1], powers[-1]))
    return powers


def sweep_forward(values, powers, tree_depth):
    for height in range(tree_depth):
        offset = 1 << height
        shifted = jnp.concatenate(
            [jnp.zeros((offset, values.shape[1]), jnp.float32), values[:-offset]], 0
        )
        values = values + apply_rows(shifted, powers[height])
    return values


def sweep_backward(values, powers, tree_depth):
    for height in range(tree_depth):
        offset = 1 << height
        shifted = jnp.concatenate(
            [values[offset:], jnp.zeros((offset, values.shape[1]), jnp.float32)], 0
        )
        values = values + apply_rows(shifted, powers[height])
    return values


def spread(anchor, powers, tree_depth):
    stacked = apply_rows(anchor[None, :], powers[0])
    for height in range(tree_depth):
        stacked = jnp.concatenate([stacked, apply_rows(stacked, powers[height])], 0)
    return stacked


def compose(earlier, latter):
    return (matmul(latter[0], earlier[0]), matmul(latter[0], earlier[1]) + latter[1])


def per_device(
    gauge_series, gauge_order, gauge_block, gauge_weight, filt_trans, obs_gain, smooth_gain
):
    states = filt_trans.shape[0]
    groups_count = lax.axis_size("tm")
    steps_dev = gauge_series.shape[0] // groups_count
    gauge_total = gauge_order.shape[0]
    count_blocks = states // gauge_weight.shape[1]
    tree_depth = steps_dev.bit_length() - 1
    position = lax.axis_index("tm")
    blocks = jnp.take(gauge_block, gauge_order)
    weights = jnp.take(gauge_weight, gauge_order, axis=0)
    onehot = (blocks[:, None] == jnp.arange(count_blocks, dtype=jnp.int32)[None, :]).astype(
        jnp.bfloat16
    )
    design = (onehot[:, :, None] * weights[:, None, :]).reshape(gauge_total, states)
    framed = gauge_series.reshape(groups_count, steps_dev, gauge_series.shape[1])
    received = lax.all_to_all(framed, "tm", split_axis=0, concat_axis=2, tiled=True)
    flattened = received.reshape(received.shape[1], received.shape[2])
    information = jnp.dot(flattened, design, preferred_element_type=jnp.float32)
    inputs = apply_rows(information, obs_gain)[None].reshape(steps_dev, states)
    filter_powers = square_table(filt_trans, tree_depth)
    local_filter = sweep_forward(inputs, filter_powers, tree_depth)
    identity = (jnp.eye(states, dtype=jnp.float32), jnp.zeros((states,), jnp.float32))
    unused_power, arrive = carried_in(
        (filter_powers[tree_depth], local_filter[-1]), "tm", compose, identity, False
    )
    filtered = local_filter + spread(arrive, filter_powers, tree_depth)
    moment = position * steps_dev + jnp.arange(steps_dev, dtype=jnp.int32)
    is_final = (moment == steps_dev * groups_count - 1)[:, None]
    blended = jnp.where(is_final, filtered, filtered - apply_rows(filtered, smooth_gain))
    smooth_powers = square_table(smooth_gain, tree_depth)
    local_smooth = sweep_backward(blended, smooth_powers, tree_depth)
    unused_back, arrive_back = carried_in(
        (smooth_powers[tree_depth], local_smooth[0]), "tm", compose, identity, True
    )
    smoothed = local_smooth + spread(arrive_back, smooth_powers, tree_depth)[::-1]
    return (filtered, smoothed)


def solution(mesh):
    placed = (
        P("groups", "tm"),
        P(),
        P(),
        P(),
        P("groups", None),
        P("groups", None),
        P("groups", None),
    )
    return jax.shard_map(
        per_device,
        mesh=mesh,
        in_specs=placed,
        out_specs=(P(("groups", "tm"), None), P(("groups", "tm"), None)),
        check_vma=False,
    )
```

profile of v0, /device:TPU:0, one launch (start us, length us, event | category | flops | bytes accessed | tf_op | source)
XLA Modules:
  0.0 216.7 jit_solution(15219739456554367077)
XLA Ops:
  7.2 1.4 fusion.83
  12.5 7.4 %all-to-all-start = ((bf16[16,64,512]{2,1,0:T(8,128)(2,1)}), bf16[16,64,512]{2,1,0:T(8,128)(2,1)}, u32[]{:S(2)}, u32[]{:S(2)}) async-start(bf16[16,64,512]{2,1,0:T(8,128)(2,1)} %bitcast.1), calls=%async_computation | async-start | bytes 2097152 | tf_op jit(solution)/shard_map/all_to_all | solution.py:96
  23.4 45.5 %gather_fusion = s32[8192]{0:T(1024)S(1)} fusion(s32[8192]{0:T(1024)S(1)} %copy-done.1, s32[8192]{0:T(1024)S(1)} %fusion.22), kind=kCustom, calls=%fused_computation | custom fusion | bytes 98304 | tf_op jit(solution)/shard_map/jit(_take)/gather | solution.py:89
  69.0 2.0 copy.13
  71.0 29.4 %gather_fusion.1 = bf16[8192,64]{1,0:T(8,128)(2,1)} fusion(bf16[8192,64]{1,0:T(8,128)(2,1)S(1)} %copy.13, s32[8192]{0:T(1024)S(1)} %fusion.22), kind=kCustom, calls=%fused_computation.1 | custom fusion | bytes 2129920 | tf_op jit(solution)/shard_map/jit(_take)/gather | solution.py:90
  100.5 5.8 %broadcast_select_fusion.2 = bf16[8192,64]{1,0:T(8,128)(2,1)S(1)} fusion(bf16[8192,64]{1,0:T(8,128)(2,1)} %gather_fusion.1, pred[8192]{0:T(1024)(128)(4,1)S(1)} %get-tuple-element.287), kind=kLoop, calls=%fused_computation.17 | loop fusion | flops 524288 | bytes 2105344 | tf_op jit(solution)/shard_map/jit(_take)/select_n | solution.py:90
  106.4 1.6 copy.14
  108.0 3.5 %broadcast_multiply_fusion = bf16[8192,4,64]{0,2,1:T(8,128)(2,1)} fusion(bf16[8192,64]{0,1:T(8,128)(2,1)} %copy.14, bf16[8192,4]{0,1:T(4,128)(2,1)S(1)} %fusion.9), kind=kLoop, calls=%fused_computation.16 | loop fusion | flops 2097152 | bytes 5308416 | tf_op jit(solution)/shard_map/mul | solution.py:94
  111.6 1.4 copy.18
  113.0 3.6 %fusion.81 = f32[256,64]{0,1:T(8,128)S(1)} fusion(bf16[8192,256]{0,1:T(8,128)(2,1)} %bitcast.133, bf16[64,8192]{1,0:T(8,128)(2,1)S(1)} %bitcast.134), kind=kOutput, calls=%fused_computation.113 | convolution fusion | flops 268435456 | bytes 5308416 | tf_op jit(solution)/shard_map/dot_general | solution.py:98
  119.3 21.8 %all-gather.2 = f32[16,1,256]{2,1,0:T(1,128)S(1)} all-gather(f32[1,1,256]{2,1,0:T(1,128)S(1)} %slice_bitcast_fusion.1), channel_id=1, replica_groups=mesh['groups'=2,'tm'=16] {'tm'}, dimensions={0}, use_global_device_ids=true | all-gather | bytes 17408 | tf_op jit(solution)/shard_map/all_gather | solution.py:11
  141.2 21.5 %while.30 = (s32[]{:T(128)}, f32[256]{0:T(256)S(1)}, s32[]{:T(128)}, f32[16,256,256]{2,1,0:T(8,128)}, f32[16,256]{1,0:T(8,128)S(1)}, /*index=5*/s32[]{:T(128)}, s32[]{:T(128)}) while((s32[]{:T(128)}, f32[256]{0:T(256)S(1)}, s32[]{:T(128)}, f32[16,256,256]{2,1,0:T(8,128)}, f32[16,256]{1,0:T(8,128)S(1)}, /*index=5*/s32[]{:T(128)}, ...), condition=%wide.region_1.2_spmd.clone, body=%wide.region_0.1_spmd.clone.sunk | while | flops 787460 | bytes 272998 | solution.py:24
  141.2 1.2 fusion.173
  145.2 1.2 fusion.173
  146.6 1.2 fusion.173
  150.6 1.2 fusion.173
  151.9 1.2 fusion.173
  156.0 1.2 fusion.173
  157.3 1.2 fusion.173
  160.0 1.2 fusion.173
  161.3 1.2 fusion.173
  167.8 17.4 %all-gather.3 = f32[16,1,256]{2,1,0:T(1,128)S(1)} all-gather(f32[1,1,256]{2,1,0:T(1,128)S(1)} %slice_bitcast_fusion), channel_id=1, replica_groups=mesh['groups'=2,'tm'=16] {'tm'}, dimensions={0}, use_global_device_ids=true | all-gather | bytes 17408 | tf_op jit(solution)/shard_map/all_gather | solution.py:11
  185.2 21.6 %while.31 = (s32[]{:T(128)}, f32[256]{0:T(256)S(1)}, s32[]{:T(128)}, f32[16,256,256]{2,1,0:T(8,128)}, f32[16,256]{1,0:T(8,128)S(1)}, /*index=5*/s32[]{:T(128)}, s32[]{:T(128)}, s32[]{:T(128)}, s32[]{:T(128)}) while((s32[]{:T(128)}, f32[256]{0:T(256)S(1)}, s32[]{:T(128)}, f32[16,256,256]{2,1,0:T(8,128)}, f32[16,256]{1,0:T(8,128)S(1)}, ...), condition=%wide.region_3.4_spmd.clone, body=%wide.region_2.3_spmd.clone.sunk | while | flops 787464 | bytes 272552 | solution.py:24
  185.2 1.2 fusion.176
  186.6 1.2 fusion.176
  187.9 1.2 fusion.176
  189.3 1.2 fusion.176
  190.6 1.2 fusion.176
  192.0 1.2 fusion.176
  193.3 1.2 fusion.176
  194.7 1.2 fusion.176
  196.0 1.2 fusion.176
  (220 shorter events, 37.6 us)
Async XLA Ops:
  7.2 12.8 %copy-start = (f32[256,256]{1,0:T(8,128)S(1)}, f32[256,256]{1,0:T(8,128)}, u32[]{:S(2)}) copy-start(f32[256,256]{1,0:T(8,128)} %param.17) | copy-start | bytes 786436
  7.2 134.0 %all-gather.7.cloned.1.call-start = ((), (), s32[]{:S(2)}) async-start(), calls=%async_computation.1 | async-start | bytes 4456448 | tf_op jit(solution)/shard_map/all_gather | solution.py:11
  8.7 0.7 copy-start.13
  9.8 1.5 copy-start.11
  10.2 0.7 copy-start.9
  11.3 8.6 %copy-start.7 = (f32[256,256]{1,0:T(8,128)}, f32[256,256]{1,0:T(8,128)S(1)}, u32[]{:S(2)}) copy-start(f32[256,256]{1,0:T(8,128)S(1)} %fusion.87) | copy-start | bytes 786436
  11.3 12.1 %copy-start.17 = (s32[8192]{0:T(1024)S(1)}, s32[8192]{0:T(1024)}, u32[]{:S(2)}) copy-start(s32[8192]{0:T(1024)} %param.12) | copy-start | bytes 98308
  11.3 12.1 %copy-start.1 = (s32[8192]{0:T(1024)S(1)}, s32[8192]{0:T(1024)}, u32[]{:S(2)}) copy-start(s32[8192]{0:T(1024)} %param.13) | copy-start | bytes 98308
  12.5 99.1 %all-to-all-start = ((bf16[16,64,512]{2,1,0:T(8,128)(2,1)}), bf16[16,64,512]{2,1,0:T(8,128)(2,1)}, u32[]{:S(2)}, u32[]{:S(2)}) async-start(bf16[16,64,512]{2,1,0:T(8,128)(2,1)} %bitcast.1), calls=%async_computation | async-start | bytes 2097152 | tf_op jit(solution)/shard_map/all_to_all | solution.py:96
  19.9 165.3 %all-gather.9.cloned.1.call-start = ((), (), s32[]{:S(2)}) async-start(), calls=%async_computation.2 | async-start | bytes 4456448 | tf_op jit(solution)/shard_map/all_gather | solution.py:11
  20.4 48.6 %copy-start.5 = (f32[256,256]{1,0:T(8,128)}, f32[256,256]{1,0:T(8,128)S(1)}, u32[]{:S(2)}) copy-start(f32[256,256]{1,0:T(8,128)S(1)} %fusion.92) | copy-start | bytes 786436
  20.8 0.7 copy-start.3
  111.5 5.1 %copy-start.15 = (f32[256,256]{1,0:T(8,128)S(1)}, f32[256,256]{1,0:T(8,128)}, u32[]{:S(2)}) copy-start(f32[256,256]{1,0:T(8,128)} %param.16) | copy-start | bytes 786436
  111.5 5.5 %copy-start.2 = (f32[256,256]{1,0:T(8,128)S(1)}, f32[256,256]{1,0:T(8,128)}, u32[]{:S(2)}) copy-start(f32[256,256]{1,0:T(8,128)} %param.15) | copy-start | bytes 786436
  111.5 5.9 %copy-start.14 = (f32[256,256]{1,0:T(8,128)S(1)}, f32[256,256]{1,0:T(8,128)}, u32[]{:S(2)}) copy-start(f32[256,256]{1,0:T(8,128)} %copy-done.13) | copy-start | bytes 786436
  111.5 6.3 %copy-start.12 = (f32[256,256]{1,0:T(8,128)S(1)}, f32[256,256]{1,0:T(8,128)}, u32[]{:S(2)}) copy-start(f32[256,256]{1,0:T(8,128)} %copy-done.11) | copy-start | bytes 786436
  111.5 6.6 %copy-start.10 = (f32[256,256]{1,0:T(8,128)S(1)}, f32[256,256]{1,0:T(8,128)}, u32[]{:S(2)}) copy-start(f32[256,256]{1,0:T(8,128)} %copy-done.9) | copy-start | bytes 786436
  113.0 6.0 %copy-start.8 = (f32[256,256]{1,0:T(8,128)S(1)}, f32[256,256]{1,0:T(8,128)}, u32[]{:S(2)}) copy-start(f32[256,256]{1,0:T(8,128)} %copy-done.7) | copy-start | bytes 786436
  116.6 49.2 %copy-start.6 = (f32[256,256]{1,0:T(8,128)S(1)}, f32[256,256]{1,0:T(8,128)}, u32[]{:S(2)}) copy-start(f32[256,256]{1,0:T(8,128)} %copy-done.5) | copy-start | bytes 786436
  117.4 48.8 %copy-start.4 = (f32[256,256]{1,0:T(8,128)S(1)}, f32[256,256]{1,0:T(8,128)}, u32[]{:S(2)}) copy-start(f32[256,256]{1,0:T(8,128)} %copy-done.3) | copy-start | bytes 786436
  165.0 44.8 %copy-start.16 = (f32[64,256]{1,0:T(8,128)}, f32[64,256]{1,0:T(8,128)S(1)}, u32[]{:S(2)}) copy-start(f32[64,256]{1,0:T(8,128)S(1)} %add.166) | copy-start | bytes 196612
Sparse Core Ops, SparseCore 0:
  12.6 65.8 all-gather.6
  80.6 49.0 all-gather.8
where the time goes:
time: 218 us; the launch traced here: 217 us
  local copies, waits for them, and re-layouts  83.9 us (38%)
  matrix products  59.5 us (27%)
  blocking collectives  39.3 us (18%)
  between operations  14.6 us (7%)
  other arithmetic  10.6 us (5%)
  starting transfers between devices  7.52 us (3%)
    dot_general x44, matrix products, matmul(): jnp.dot(left, right, precision=PRECISE, preferred_element_type=jnp.float32)  46.2 us
    gather x1, local copies, waits for them, and re-layouts, per_device(): blocks = jnp.take(gauge_block, gauge_order)  45.5 us
    all_gather x2, blocking collectives, carried_in(): everything = jax.tree.map(lambda part: lax.all_gather(part, axis), array)  39.3 us
    gather x1, local copies, waits for them, and re-layouts, per_device(): weights = jnp.take(gauge_weight, gauge_order, axis=0)  29.4 us
    dot_general x28, matrix products, apply_rows(): lax.dot_general(values, matrix, (((1,), (1,)), ((), ())), precision=PRECI...  9.56 us
    all_to_all x1, starting transfers between devices, per_device(): lax.all_to_all(framed, 'tm', split_axis=0, concat_axis=2, tiled=True)  7.44 us
    select_n x1, other arithmetic, per_device(): weights = jnp.take(gauge_weight, gauge_order, axis=0)  5.83 us
    unnamed x42, local copies, waits for them, and re-layouts  4.86 us
  transfers between devices with their start and end apart: 3, of which 0 were waited for; matrix products, arithmetic and copies ran while one was open for 57% of the time, Pallas kernels for 0%

commit v1 on v0

v1 whole, which is shorter than its diff:
```python
import jax
import jax.numpy as jnp
from jax import lax
from jax.sharding import PartitionSpec as P

PRECISE = lax.Precision.HIGHEST


def matmul(left, right):
    return jnp.dot(left, right, precision=PRECISE, preferred_element_type=jnp.float32)


def shift_down(values, offset):
    zeros = jnp.zeros((offset, values.shape[1]), jnp.float32)
    return jnp.concatenate([zeros, values[:-offset]], 0)


def shift_up(values, offset):
    zeros = jnp.zeros((offset, values.shape[1]), jnp.float32)
    return jnp.concatenate([values[offset:], zeros], 0)


def sweep(values, powers, shift):
    for height, power in enumerate(powers):
        values = values + matmul(shift(values, 1 << height), power)
    return values


def per_device(
    gauge_series, gauge_order, gauge_block, gauge_weight, filt_trans, obs_gain, smooth_gain
):
    states = filt_trans.shape[0]
    devices = lax.axis_size("tm")
    steps = gauge_series.shape[0]
    steps_dev = steps // devices
    columns = gauge_series.shape[1]
    block = gauge_weight.shape[1]
    count_blocks = states // block
    tree_depth = steps_dev.bit_length() - 1
    scan_depth = devices.bit_length() - 1
    position = lax.axis_index("tm")

    mine = lax.dynamic_slice(gauge_order, (position * columns,), (columns,))
    blocks = gauge_block.at[mine].get(mode="promise_in_bounds")
    weights = gauge_weight.at[mine].get(mode="promise_in_bounds")
    chosen = blocks[:, None, None] == jnp.arange(count_blocks, dtype=jnp.int32)[None, :, None]
    design = jnp.where(chosen, weights[:, None, :], jnp.bfloat16(0)).reshape(columns, states)
    information = jnp.dot(gauge_series, design, preferred_element_type=jnp.float32)

    gain = obs_gain.T
    filt = [filt_trans.T]
    back = [smooth_gain.T]
    enter = filt[0] - matmul(filt[0], back[0])
    crossed = []
    for height in range(tree_depth):
        pair = matmul(jnp.concatenate([enter, back[-1]], 0), back[-1])
        crossed.append(pair[:states])
        back.append(pair[states:])
        wide = matmul(filt[-1], jnp.concatenate([filt[-1], crossed[-1]], 1))
        filt.append(wide[:, :states])
        enter = enter + wide[:, states:]
    for height in range(scan_depth - 1):
        filt.append(matmul(filt[-1], filt[-1]))
        back.append(matmul(back[-1], back[-1]))

    ends = matmul(information, gain)
    starts = ends - matmul(ends, back[0])
    for height in range(tree_depth):
        ends = ends.reshape(-1, 2, states)
        starts = starts.reshape(-1, 2, states)
        wide = matmul(ends[:, 0], jnp.concatenate([filt[height], crossed[height]], 1))
        starts = starts[:, 0] + wide[:, states:] + matmul(starts[:, 1], back[height])
        ends = ends[:, 1] + wide[:, :states]

    reached = sweep(ends, filt[tree_depth : tree_depth + scan_depth], shift_down)
    arrive = shift_down(reached, 1)
    final = reached[-1:]
    starts = starts + matmul(arrive, enter)
    last = jnp.zeros((devices - 1, states), jnp.float32)
    starts = starts + jnp.concatenate([last, matmul(final, back[tree_depth])], 0)
    returned = sweep(starts, back[tree_depth : tree_depth + scan_depth], shift_up)
    arrive_back = jnp.concatenate([returned[1:], final], 0)

    packed = jnp.concatenate(
        [
            information.reshape(devices, steps_dev, states),
            arrive[:, None],
            arrive_back[:, None],
            jnp.zeros((devices, 6, states), jnp.float32),
        ],
        1,
    )
    parts = lax.all_to_all(packed, "tm", split_axis=0, concat_axis=0, tiled=True)
    total = jnp.sum(parts, 0)
    entering = total[steps_dev : steps_dev + 1]
    entering_back = total[steps_dev + 1 : steps_dev + 2]

    inputs = matmul(total[:steps_dev], gain)
    inputs = inputs + jnp.concatenate(
        [matmul(entering, filt[0]), jnp.zeros((steps_dev - 1, states), jnp.float32)], 0
    )
    filtered = sweep(inputs, filt[:tree_depth], shift_down)
    following = jnp.concatenate(
        [jnp.zeros((steps_dev - 1, states), jnp.float32), entering_back], 0
    )
    blended = filtered + matmul(following - filtered, back[0])
    smoothed = sweep(blended, back[:tree_depth], shift_up)
    return (filtered, smoothed)


def solution(mesh):
    placed = (
        P("groups", "tm"),
        P(),
        P(),
        P(),
        P("groups", None),
        P("groups", None),
        P("groups", None),
    )
    return jax.shard_map(
        per_device,
        mesh=mesh,
        in_specs=placed,
        out_specs=(P(("groups", "tm"), None), P(("groups", "tm"), None)),
        check_vma=False,
    )
```

time: 218 us -> 130 us (0.60)
  local copies, waits for them, and re-layouts: 83.9 us -> 43.8 us
  matrix products: 59.5 us -> 40.4 us
  between operations: 14.6 us -> 2.07 us
  starting transfers between devices: 7.52 us -> 0 us
  other arithmetic: 10.6 us -> 6.51 us
  blocking collectives: 39.3 us -> 36.8 us
    gather x2 -> x3, local copies, waits for them, and re-layouts: 75 us -> 4.58 us  [the longest x1 3.14 us: per_device(): blocks = gauge_block.at[mine].get(mode='promise_in_bounds')]
    all_gather x2 -> x0, blocking collectives: 39.3 us -> none  [carried_in(): everything = jax.tree.map(lambda part: lax.all_gather(part, axis), array)]
    all_to_all x0 -> x1, blocking collectives: none -> 36.8 us  [per_device(): lax.all_to_all(packed, 'tm', split_axis=0, concat_axis=0, tiled=True)]
    dot_general x29 -> x1, matrix products: 13.2 us -> 0.46 us  [per_device(): jnp.dot(gauge_series, design, preferred_element_type=jnp.float32)]
    reshape x0 -> x12, local copies, waits for them, and re-layouts: none -> 12.6 us  [the longest x6 6.92 us: per_device(): starts = starts.reshape(-1, 2, states)]
    slice x9 -> x35, local copies, waits for them, and re-layouts: 0.06 us -> 10.5 us  [the longest x6 5.68 us: per_device(): starts[:, 1]]
    unnamed x42 -> x116, local copies, waits for them, and re-layouts: 4.86 us -> 14.6 us
    all_to_all x1 -> x0, starting transfers between devices: 7.44 us -> none  [per_device(): lax.all_to_all(framed, 'tm', split_axis=0, concat_axis=2, tiled=True)]
  transfers between devices with their start and end apart: 3 -> 0, of which waited for: 0 -> 0; matrix products, arithmetic and copies ran while one was open for 57% -> 0% of each run, Pallas kernels for 0% -> 0%
where the time goes in v1:
time: 130 us; the launch traced here: 129 us
  local copies, waits for them, and re-layouts  43.8 us (34%)
  matrix products  40.4 us (31%)
  blocking collectives  36.8 us (28%)
  other arithmetic  6.51 us (5%)
  between operations  2.07 us (2%)
    dot_general x58, matrix products, matmul(): jnp.dot(left, right, precision=PRECISE, preferred_element_type=jnp.float32)  39.9 us
    all_to_all x1, blocking collectives, per_device(): lax.all_to_all(packed, 'tm', split_axis=0, concat_axis=0, tiled=True)  36.8 us
    unnamed x116, local copies, waits for them, and re-layouts  14.6 us
    reshape x6, local copies, waits for them, and re-layouts, per_device(): starts = starts.reshape(-1, 2, states)  6.92 us
    reshape x6, local copies, waits for them, and re-layouts, per_device(): ends = ends.reshape(-1, 2, states)  5.7 us
    slice x6, local copies, waits for them, and re-layouts, per_device(): starts[:, 1]  5.68 us
    slice x6, local copies, waits for them, and re-layouts, per_device(): ends = ends[:, 1] + wide[:, :states]  3.94 us
    gather x1, local copies, waits for them, and re-layouts, per_device(): blocks = gauge_block.at[mine].get(mode='promise_in_bounds')  3.14 us

profile of v1, /device:TPU:0, one launch (start us, length us, event | category | flops | bytes accessed | tf_op | source)
XLA Modules:
  0.0 129.5 jit_solution(2229440213275140554)
XLA Ops:
  1.5 2.0 %copy.27 = bf16[8192,64]{1,0:T(8,128)(2,1)S(1)} copy(bf16[8192,64]{0,1:T(8,128)(2,1)} %param.10) | data formatting | bytes 2097152 | tf_op args[3]
  3.5 1.3 %gather_fusion.1 = bf16[512,64]{1,0:T(8,128)(2,1)S(1)} fusion(bf16[8192,64]{1,0:T(8,128)(2,1)S(1)} %copy.27, s32[1024]{0:T(1024)S(1)} %pad_clamp_fusion), kind=kCustom, calls=%fused_computation.1 | custom fusion | bytes 133120 | tf_op jit(solution)/shard_map/gather | solution.py:45
  5.0 3.1 %gather_fusion = s32[512]{0:T(512)S(1)} fusion(s32[8192]{0:T(1024)S(1)} %copy-done.1, s32[1024]{0:T(1024)S(1)} %pad_clamp_fusion), kind=kCustom, calls=%fused_computation | custom fusion | bytes 6144 | tf_op jit(solution)/shard_map/gather | solution.py:44
  9.2 1.8 %fusion.174 = f32[1024,256]{1,0:T(8,128)S(1)} fusion(f32[256,1024]{1,0:T(8,128)S(1)} %fusion.173, f32[256,256]{1,0:T(8,128)S(1)} %copy-done.46), kind=kOutput, calls=%fused_computation.252 | convolution fusion | flops 805306368 | bytes 2359296 | tf_op jit(solution)/shard_map/dot_general | solution.py:10
  11.0 1.6 %reshape.83 = f32[512,2,256]{2,1,0:T(2,128)} reshape(f32[1024,256]{1,0:T(8,128)S(1)} %fusion.174) | data formatting | bytes 2097152 | tf_op jit(solution)/shard_map/reshape | solution.py:69
  13.4 2.0 %convolution_subtract_fusion = f32[1024,256]{1,0:T(8,128)} fusion(f32[1024,256]{1,0:T(8,128)S(1)} %fusion.174, f32[256,256]{1,0:T(8,128)S(1)} %copy-done.2), kind=kOutput, calls=%fused_computation.2 | convolution fusion | flops 805568512 | bytes 2359296 | tf_op jit(solution)/shard_map/dot_general | solution.py:10
  16.5 1.6 %convolution_subtract_fusion.1 = f32[256,256]{1,0:T(8,128)S(1)} fusion(f32[256,256]{1,0:T(8,128)} %param.11, f32[256,256]{1,0:T(8,128)S(1)} %copy-done.2, f32[256,256]{0,1:T(8,128)S(1)} %copy.31), kind=kOutput, calls=%fused_computation.7 | convolution fusion | flops 201392128 | bytes 1048576 | tf_op jit(solution)/shard_map/dot_general | solution.py:10
  31.7 1.5 %fusion.47 = f32[256,256]{1,0:T(8,128)} fusion(f32[512,256]{0,1:T(8,128)S(1)} %fusion.29), kind=kOutput, calls=%fused_computation.102 | convolution fusion | flops 201326592 | bytes 524288 | tf_op jit(solution)/shard_map/dot_general | solution.py:10
  36.9 2.2 %reshape.84 = f32[256,2,256]{2,1,0:T(2,128)} reshape(f32[512,256]{1,0:T(8,128)} %slice_add_fusion.1) | data formatting | bytes 1048576 | tf_op jit(solution)/shard_map/reshape | solution.py:69
  39.1 1.7 %fusion.154 = (f32[256,1,256]{2,1,0:T(1,128)S(1)}, f32[256,1,256]{2,1,0:T(1,128)S(1)}) fusion(f32[256,2,256]{2,1,0:T(2,128)} %reshape.84), kind=kLoop, calls=%fused_computation.232 | loop fusion | bytes 1048576 | tf_op jit(solution)/shard_map/slice | solution.py:73
  43.0 1.8 %reshape.85 = f32[128,2,256]{2,1,0:T(2,128)} reshape(f32[256,256]{1,0:T(8,128)} %slice_add_fusion.9) | data formatting | bytes 524288 | tf_op jit(solution)/shard_map/reshape | solution.py:69
  44.8 1.3 fusion.166
  46.0 1.4 %fusion.16 = f32[128,512]{1,0:T(8,128)S(1)} fusion(f32[256,256]{1,0:T(8,128)} %copy-done.38, f32[256,256]{1,0:T(8,128)S(1)} %copy-done.31, f32[128,1,256]{2,1,0:T(1,128)S(1)} %get-tuple-element.33), kind=kOutput, calls=%fused_computation.55 | convolution fusion | flops 201457664 | bytes 917504 | tf_op jit(solution)/shard_map/dot_general | solution.py:10
  48.4 1.5 %fusion.22 = f32[64,512]{1,0:T(8,128)S(1)} fusion(f32[256,256]{1,0:T(8,128)} %copy-done.43, f32[256,256]{1,0:T(8,128)} %copy-done.37, f32[64,1,256]{2,1,0:T(1,128)S(1)} %get-tuple-element.37), kind=kOutput, calls=%fused_computation.62 | convolution fusion | flops 100794368 | bytes 720896 | tf_op jit(solution)/shard_map/dot_general | solution.py:10
  50.6 1.4 %fusion.28 = f32[32,512]{1,0:T(8,128)S(1)} fusion(f32[256,256]{1,0:T(8,128)} %copy-done.42, f32[256,256]{1,0:T(8,128)} %copy-done.36, f32[32,1,256]{2,1,0:T(1,128)S(1)} %get-tuple-element.41), kind=kOutput, calls=%fused_computation.69 | convolution fusion | flops 50462720 | bytes 622592 | tf_op jit(solution)/shard_map/dot_general | solution.py:10
  53.6 1.8 %fusion.33 = f32[256,512]{1,0:T(8,128)S(1)} fusion(f32[256,256]{1,0:T(8,128)} %get-tuple-element.10, f32[256,256]{1,0:T(8,128)} %copy.65), kind=kOutput, calls=%fused_computation.75 | convolution fusion | flops 402784256 | bytes 1048576 | tf_op jit(solution)/shard_map/dot_general | solution.py:10
  59.5 2.8 %reshape.89 = f32[512,2,256]{2,1,0:T(2,128)} reshape(f32[1024,256]{1,0:T(8,128)} %convolution_subtract_fusion) | data formatting | bytes 2097152 | tf_op jit(solution)/shard_map/reshape | solution.py:70
  62.3 2.5 %fusion.151 = (f32[512,1,256]{2,1,0:T(1,128)S(1)}, f32[512,1,256]{2,1,0:T(1,128)S(1)}) fusion(f32[512,2,256]{2,1,0:T(2,128)} %reshape.89), kind=kLoop, calls=%fused_computation.229 | loop fusion | bytes 2097152 | tf_op jit(solution)/shard_map/slice | solution.py:72
  64.9 1.5 %convolution_add_fusion = f32[512,256]{1,0:T(8,128)} fusion(f32[256,256]{1,0:T(8,128)S(1)} %copy-done.2, f32[512,512]{1,0:T(8,128)S(1)} %copy-done.16, f32[512,1,256]{2,1,0:T(1,128)S(1)} %get-tuple-element.3, f32[512,1,256]{2,1,0:T(1,128)S(1)} %get-tuple-element.2), kind=kOutput, calls=%fused_computation.4 | convolution fusion | flops 402915328 | bytes 2359296 | tf_op jit(solution)/shard_map/dot_general | solution.py:10
  66.3 2.1 %reshape.90 = f32[256,2,256]{2,1,0:T(2,128)} reshape(f32[512,256]{1,0:T(8,128)} %convolution_add_fusion) | data formatting | bytes 1048576 | tf_op jit(solution)/shard_map/reshape | solution.py:70
  68.5 1.7 %fusion.153 = (f32[256,1,256]{2,1,0:T(1,128)S(1)}, f32[256,1,256]{2,1,0:T(1,128)S(1)}) fusion(f32[256,2,256]{2,1,0:T(2,128)} %reshape.90), kind=kLoop, calls=%fused_computation.231 | loop fusion | bytes 1048576 | tf_op jit(solution)/shard_map/slice | solution.py:72
  71.3 1.8 %reshape.91 = f32[128,2,256]{2,1,0:T(2,128)} reshape(f32[256,256]{1,0:T(8,128)} %convolution_add_fusion.1) | data formatting | bytes 524288 | tf_op jit(solution)/shard_map/reshape | solution.py:70
  73.1 1.3 fusion.165
  74.4 1.5 %convolution_add_fusion.2 = f32[128,256]{1,0:T(8,128)S(1)} fusion(f32[128,512]{1,0:T(8,128)S(1)} %copy-done.49, f32[128,1,256]{2,1,0:T(1,128)S(1)} %get-tuple-element.31, f32[128,1,256]{2,1,0:T(1,128)S(1)} %get-tuple-element.30, f32[512,256]{1,0:T(8,128)} %copy-done.4), kind=kOutput, calls=%fused_computation.8 | convolution fusion | flops 100728832 | bytes 786432 | tf_op jit(solution)/shard_map/dot_general | solution.py:10
  76.0 1.2 convolution_add_fusion.17
  77.3 1.2 convolution_add_fusion.18
  78.6 1.2 convolution_add_fusion.23
  79.9 1.3 fusion
  83.1 1.3 %copy.29 = f32[1024,256]{1,0:T(8,128)} copy(f32[1024,256]{0,1:T(8,128)S(1)} %bitcast.153) | data formatting | bytes 2097152 | tf_op jit(solution)/shard_map/dot_general | solution.py:48
  84.5 1.4 %maximum_maximum_fusion = f32[16,72,256]{2,1,0:T(8,128)S(1)} fusion(f32[16,1,256]{2,1,0:T(1,128)S(1)} %copy.46, f32[16,1,256]{2,1,0:T(1,128)S(1)} %copy.45, f32[16,64,256]{2,1,0:T(8,128)} %bitcast.154, f32[72]{0:T(128)S(1)} %pad.27.clone), kind=kLoop, calls=%fused_computation.5 | loop fusion | flops 884736 | bytes 2261280 | tf_op jit(solution)/shard_map/concatenate | solution.py:84
  85.9 36.8 %all_to_all.5 = f32[16,72,256]{2,1,0:T(8,128)} all-to-all(f32[16,72,256]{2,1,0:T(8,128)S(1)} %maximum_maximum_fusion), channel_id=1, replica_groups=mesh['groups'=2,'tm'=16] {'tm'}, dimensions={0} | all-to-all | bytes 2359296 | tf_op jit(solution)/shard_map/all_to_all | solution.py:93
  122.7 1.4 %reduce_sum.9 = f32[72,256]{1,0:T(8,128)S(1)} reduce(f32[16,72,256]{2,1,0:T(8,128)} %all_to_all.5, f32[]{:T(128)} %constant.11.clone.1), dimensions={0}, to_apply=%region_0.1 | reduce | flops 276480 | bytes 1253380 | tf_op jit(solution)/shard_map/reduce_sum | solution.py:94
  (219 shorter events, 38.4 us)
Async XLA Ops:
  0.6 7.6 %copy-start = (bf16[1024,512]{1,0:T(8,128)(2,1)S(1)}, bf16[1024,512]{1,0:T(8,128)(2,1)}, u32[]{:S(2)}) copy-start(bf16[1024,512]{1,0:T(8,128)(2,1)} %param.7) | copy-start | bytes 3145732
  11.0 1.6 %copy-start.2 = (f32[256,256]{1,0:T(8,128)S(1)}, f32[256,256]{1,0:T(8,128)}, u32[]{:S(2)}) copy-start(f32[256,256]{1,0:T(8,128)} %param.13) | copy-start | bytes 786436
  16.5 1.6 %copy-start.50 = (f32[256,256]{0,1:T(8,128)S(1)}, f32[256,256]{0,1:T(8,128)}, u32[]{:S(2)}) copy-start(f32[256,256]{0,1:T(8,128)} %copy.32) | copy-start | bytes 786436
  19.8 2.8 %copy-start.32 = (f32[256,256]{1,0:T(8,128)}, f32[256,256]{1,0:T(8,128)S(1)}, u32[]{:S(2)}) copy-start(f32[256,256]{1,0:T(8,128)S(1)} %get-tuple-element.26) | copy-start | bytes 786436
  21.2 4.4 %copy-start.4 = (f32[512,256]{1,0:T(8,128)}, f32[512,256]{1,0:T(8,128)S(1)}, u32[]{:S(2)}) copy-start(f32[512,256]{1,0:T(8,128)S(1)} %fusion.5) | copy-start | bytes 1572868
  22.7 2.8 %copy-start.30 = (f32[256,256]{1,0:T(8,128)}, f32[256,256]{1,0:T(8,128)S(1)}, u32[]{:S(2)}) copy-start(f32[256,256]{1,0:T(8,128)S(1)} %get-tuple-element.22) | copy-start | bytes 786436
  24.1 3.8 %copy-start.6 = (f32[512,256]{1,0:T(8,128)}, f32[512,256]{1,0:T(8,128)S(1)}, u32[]{:S(2)}) copy-start(f32[512,256]{1,0:T(8,128)S(1)} %fusion.11) | copy-start | bytes 1572868
  25.6 2.1 %copy-start.37 = (f32[256,256]{1,0:T(8,128)}, f32[256,256]{1,0:T(8,128)S(1)}, u32[]{:S(2)}) copy-start(f32[256,256]{1,0:T(8,128)S(1)} %get-tuple-element.18) | copy-start | bytes 786436
  26.3 3.8 %copy-start.8 = (f32[512,256]{1,0:T(8,128)}, f32[512,256]{1,0:T(8,128)S(1)}, u32[]{:S(2)}) copy-start(f32[512,256]{1,0:T(8,128)S(1)} %fusion.17) | copy-start | bytes 1572868
  28.6 1.5 %copy-start.13 = (f32[512,256]{1,0:T(8,128)}, f32[512,256]{1,0:T(8,128)S(1)}, u32[]{:S(2)}) copy-start(f32[512,256]{1,0:T(8,128)S(1)} %fusion.23) | copy-start | bytes 1572868
  29.3 1.5 %copy-start.28 = (f32[256,512]{1,0:T(8,128)}, f32[256,512]{1,0:T(8,128)S(1)}, u32[]{:S(2)}) copy-start(f32[256,512]{1,0:T(8,128)S(1)} %fusion.27) | copy-start | bytes 1572868
  30.2 3.0 %copy-start.17 = (f32[512,2,256]{2,1,0:T(2,128)S(1)}, f32[512,2,256]{2,1,0:T(2,128)}, u32[]{:S(2)}) copy-start(f32[512,2,256]{2,1,0:T(2,128)} %reshape.83) | copy-start | bytes 3145732
  36.9 3.9 %copy-start.33 = (f32[256,256]{1,0:T(8,128)S(1)}, f32[256,256]{1,0:T(8,128)}, u32[]{:S(2)}) copy-start(f32[256,256]{1,0:T(8,128)} %copy-done.32) | copy-start | bytes 786436
  39.1 1.7 %copy-start.40 = (f32[256,256]{1,0:T(8,128)S(1)}, f32[256,256]{1,0:T(8,128)}, u32[]{:S(2)}) copy-start(f32[256,256]{1,0:T(8,128)} %copy-done.39) | copy-start | bytes 786436
  41.4 4.6 %copy-start.31 = (f32[256,256]{1,0:T(8,128)S(1)}, f32[256,256]{1,0:T(8,128)}, u32[]{:S(2)}) copy-start(f32[256,256]{1,0:T(8,128)} %copy-done.30) | copy-start | bytes 786436
  48.2 4.5 %slice-start = ((f32[512,256]{0,1:T(8,128)}), f32[256,256]{0,1:T(8,128)S(1)}, s32[]{:S(2)}) async-start(f32[512,256]{0,1:T(8,128)} %copy-done.10), calls=%async_computation.1 | async-start | bytes 524288 | tf_op jit(solution)/shard_map/slice | solution.py:57
  53.6 1.8 %copy-start.35 = (f32[256,256]{1,0:T(8,128)S(1)}, f32[256,256]{1,0:T(8,128)}, u32[]{:S(2)}) copy-start(f32[256,256]{1,0:T(8,128)} %get-tuple-element.10) | copy-start | bytes 786436
  53.6 1.8 %copy-start.41 = (f32[256,256]{1,0:T(8,128)S(1)}, f32[256,256]{1,0:T(8,128)}, u32[]{:S(2)}) copy-start(f32[256,256]{1,0:T(8,128)} %copy.65) | copy-start | bytes 786436
  55.4 1.9 %copy-start.27 = (f32[256,512]{1,0:T(8,128)}, f32[256,512]{1,0:T(8,128)S(1)}, u32[]{:S(2)}) copy-start(f32[256,512]{1,0:T(8,128)S(1)} %fusion.33) | copy-start | bytes 1572868
  56.6 1.5 %copy-start.11 = (f32[512,256]{0,1:T(8,128)S(1)}, f32[512,256]{0,1:T(8,128)}, u32[]{:S(2)}) copy-start(f32[512,256]{0,1:T(8,128)} %copy-done.10) | copy-start | bytes 1572868
  62.3 2.5 %copy-start.16 = (f32[512,512]{1,0:T(8,128)S(1)}, f32[512,512]{1,0:T(8,128)}, u32[]{:S(2)}) copy-start(f32[512,512]{1,0:T(8,128)} %copy-done.15) | copy-start | bytes 3145732
  68.5 1.7 %copy-start.45 = (f32[256,512]{1,0:T(8,128)S(1)}, f32[256,512]{1,0:T(8,128)}, u32[]{:S(2)}) copy-start(f32[256,512]{1,0:T(8,128)} %copy-done.44) | copy-start | bytes 1572868
  70.2 4.2 %copy-start.49 = (f32[128,512]{1,0:T(8,128)S(1)}, f32[128,512]{1,0:T(8,128)}, u32[]{:S(2)}) copy-start(f32[128,512]{1,0:T(8,128)} %copy-done.48) | copy-start | bytes 786436
  77.2 4.3 %copy-start.18 = (f32[256,256]{1,0:T(8,128)S(1)}, f32[256,256]{1,0:T(8,128)}, u32[]{:S(2)}) copy-start(f32[256,256]{1,0:T(8,128)} %fusion.47) | copy-start | bytes 786436
  78.6 2.6 %copy-start.12 = (f32[512,256]{0,1:T(8,128)S(1)}, f32[512,256]{0,1:T(8,128)}, u32[]{:S(2)}) copy-start(f32[512,256]{0,1:T(8,128)} %copy-done.10) | copy-start | bytes 1572868
  81.5 1.5 %copy-start.55 = (f32[1,256]{1,0:T(1,128)S(1)}, f32[1,256]{1,0:T(1,128)}, u32[]{:S(2)}) copy-start(f32[1,256]{1,0:T(1,128)} %slice.412) | copy-start | bytes 3076
  122.7 1.8 %copy-start.47 = (f32[256,256]{1,0:T(8,128)S(1)}, f32[256,256]{1,0:T(8,128)}, u32[]{:S(2)}) copy-start(f32[256,256]{1,0:T(8,128)} %param.12) | copy-start | bytes 786436
  122.7 2.6 %copy-start.20 = (f32[256,512]{1,0:T(8,128)S(1)}, f32[256,512]{1,0:T(8,128)}, u32[]{:S(2)}) copy-start(f32[256,512]{1,0:T(8,128)} %copy-done.19) | copy-start | bytes 1572868
  122.7 2.8 %copy-start.22 = (f32[256,512]{1,0:T(8,128)S(1)}, f32[256,512]{1,0:T(8,128)}, u32[]{:S(2)}) copy-start(f32[256,512]{1,0:T(8,128)} %copy-done.21) | copy-start | bytes 1572868
  124.1 1.7 %copy-start.24 = (f32[256,512]{1,0:T(8,128)S(1)}, f32[256,512]{1,0:T(8,128)}, u32[]{:S(2)}) copy-start(f32[256,512]{1,0:T(8,128)} %copy-done.23) | copy-start | bytes 1572868
  124.5 1.6 %copy-start.26 = (f32[256,512]{1,0:T(8,128)S(1)}, f32[256,512]{1,0:T(8,128)}, u32[]{:S(2)}) copy-start(f32[256,512]{1,0:T(8,128)} %copy-done.25) | copy-start | bytes 1572868
  126.6 1.6 %copy-start.53 = (f32[64,256]{1,0:T(8,128)}, f32[64,256]{1,0:T(8,128)S(1)}, u32[]{:S(2)}) copy-start(f32[64,256]{1,0:T(8,128)S(1)} %convolution_add_fusion.10) | copy-start | bytes 196612
  (25 other events, 23.9 us)

commit v2 on v1

v2 whole, which is shorter than its diff:
```python
import functools

import jax
import jax.numpy as jnp
from jax import lax
from jax.experimental import pallas as pl
from jax.experimental.pallas import tpu as pltpu
from jax.sharding import PartitionSpec as P

PRECISE = lax.Precision.HIGHEST
MESH = pl.DeviceIdType.MESH
LANES = 128


def matmul(left, right):
    return jnp.dot(left, right, precision=PRECISE, preferred_element_type=jnp.float32)


def shift(values, offset):
    rows = values.shape[0]
    moved = pltpu.roll(values, offset % rows, 0)
    place = lax.broadcasted_iota(jnp.int32, values.shape, 0)
    kept = place >= offset if offset > 0 else place < rows + offset
    return jnp.where(kept, moved, 0.0)


def put_row(values, row, where):
    place = lax.broadcasted_iota(jnp.int32, values.shape, 0)
    return values + jnp.where(place == where, row, 0.0)


def bit_reversed(number, bits):
    return int(format(number, "b").zfill(bits)[::-1], 2) if bits else 0


def kernel(
    devices,
    series_ref,
    order_ref,
    block_ref,
    weight_ref,
    filt_in,
    gain_in,
    back_in,
    filtered_ref,
    smoothed_ref,
    info,
    half,
    land,
    carry,
    carry_land,
    filt,
    back,
    crossed,
    enter,
    gain,
    ends,
    starts,
    small,
    sib_send,
    sib_recv,
    info_send,
    info_recv,
    carry_send,
    carry_recv,
):
    me = lax.axis_index("tm")
    core = lax.rem(me, 2)
    chip = lax.div(me, 2)
    sibling = me + 1 - 2 * core
    chips = devices // 2
    steps = series_ref.shape[0]
    length = steps // devices
    states = filt_in.shape[0]
    gauges = weight_ref.shape[1]
    block = weight_ref.shape[0]
    depth = length.bit_length() - 1
    scans = devices.bit_length() - 1
    halves = states // LANES

    barrier = pltpu.get_barrier_semaphore()
    for k in range(1, devices):
        pl.semaphore_signal(
            barrier, inc=1, device_id={"tm": lax.rem(me + k, devices)}, device_id_type=MESH
        )

    order = order_ref[me]
    piece = min(1024, gauges)
    gathered = None
    for base in range(0, gauges, piece):
        spot = lax.broadcasted_iota(jnp.int32, (piece, order.shape[1]), 0) + base
        onehot = jnp.where(spot == order, 1.0, 0.0).astype(jnp.bfloat16)
        blocks = block_ref[:, base : base + piece].astype(jnp.float32)
        blocks = jnp.broadcast_to(blocks, (16, piece)).astype(jnp.bfloat16)
        table = jnp.concatenate([weight_ref[:, base : base + piece], blocks], 0)
        part = jnp.dot(table, onehot, preferred_element_type=jnp.float32)
        gathered = part if gathered is None else gathered + part
    weights = gathered[:block]
    number = gathered[block : block + 1]
    design = jnp.concatenate(
        [jnp.where(number == float(k), weights, 0.0) for k in range(states // block)], 0
    ).astype(jnp.bfloat16)
    chunk = min(steps, 1024)
    for base in range(0, steps, chunk):
        partial = lax.dot_general(
            series_ref[base : base + chunk],
            design,
            (((1,), (1,)), ((), ())),
            preferred_element_type=jnp.float32,
        )
        for b in range(base // length, (base + chunk) // length):
            at = ((b % 2) * chips + b // 2) * length
            row = b * length - base
            for j in range(halves):
                info[j, at : at + length] = partial[
                    row : row + length, j * LANES : (j + 1) * LANES
                ]

    pl.semaphore_wait(barrier, devices - 1)
    sib = []
    for k in range(chips):
        target = lax.rem(chip + k, chips)
        rows = pl.ds(pl.multiple_of(((1 - core) * chips + target) * length, length), length)
        copy = pltpu.make_async_remote_copy(
            src_ref=info.at[:, rows],
            dst_ref=half.at[k],
            send_sem=sib_send.at[k],
            recv_sem=sib_recv.at[k],
            device_id={"tm": sibling},
            device_id_type=MESH,
        )
        copy.start()
        sib.append(copy)

    for t in range(length):
        at = bit_reversed(t, depth) * devices
        for c in range(2):
            for j in range(halves):
                ends[at + c * chips : at + (c + 1) * chips, j * LANES : (j + 1) * LANES] = info[
                    j, pl.ds(c * chips * length + t, chips, stride=length)
                ]

    gain[...] = gain_in[...].T
    filt[0] = filt_in[...].T
    back[0] = back_in[...].T
    enter[...] = filt[0] - matmul(filt[0], back[0])

    sends = []
    for k in range(chips):
        sib[k].wait()
        target = lax.rem(chip + k, chips)
        rows = pl.ds(pl.multiple_of((core * chips + target) * length, length), length)
        half[k] = half[k] + info[:, rows]
        if k > 0:
            copy = pltpu.make_async_remote_copy(
                src_ref=half.at[k],
                dst_ref=land.at[k],
                send_sem=info_send.at[k],
                recv_sem=info_recv.at[k],
                device_id={"tm": 2 * target + core},
                device_id_type=MESH,
            )
            copy.start()
            sends.append(copy)

    for h in range(depth):
        crossed[h] = matmul(enter[...], back[h])
        back[h + 1] = matmul(back[h], back[h])
        filt[h + 1] = matmul(filt[h], filt[h])
        enter[...] = enter[...] + matmul(filt[h], crossed[h])
    for h in range(depth, depth + scans - 1):
        filt[h + 1] = matmul(filt[h], filt[h])
        back[h + 1] = matmul(back[h], back[h])

    for base in range(0, steps, chunk):
        here = slice(base, base + chunk)
        ends[here] = matmul(ends[here], gain[...])
        starts[here] = ends[here] - matmul(ends[here], back[0])
    rows = steps
    for h in range(depth):
        rows //= 2
        part = min(rows, chunk)
        for base in range(0, rows, part):
            here = slice(base, base + part)
            there = slice(rows + base, rows + base + part)
            left = ends[here]
            starts[here] = (
                starts[here] + matmul(starts[there], back[h]) + matmul(left, crossed[h])
            )
            ends[here] = ends[there] + matmul(left, filt[h])

    for b in range(devices):
        source = (b % 2) * chips + b // 2
        small[0, b : b + 1] = ends[source : source + 1]
        small[1, b : b + 1] = starts[source : source + 1]
    reached = small[0]
    opened = small[1]
    for h in range(scans):
        reached = reached + matmul(shift(reached, 1 << h), filt[depth + h])
    arrive = shift(reached, 1)
    final = reached[devices - 1 : devices]
    opened = opened + matmul(arrive, enter[...])
    leaving = put_row(jnp.zeros_like(opened), final, devices - 1)
    opened = opened + matmul(leaving, back[depth])
    for h in range(scans):
        opened = opened + matmul(shift(opened, -(1 << h)), back[depth + h])
    arrive_back = put_row(shift(opened, -1), final, devices - 1)
    for b in range(devices):
        carry[b, 0:1] = arrive[b : b + 1]
        carry[b, 1:2] = arrive_back[b : b + 1]

    carries = []
    for k in range(1, devices):
        target = lax.rem(me + k, devices)
        copy = pltpu.make_async_remote_copy(
            src_ref=carry.at[target],
            dst_ref=carry_land.at[k],
            send_sem=carry_send.at[k],
            recv_sem=carry_recv.at[k],
            device_id={"tm": target},
            device_id_type=MESH,
        )
        copy.start()
        carries.append(copy)

    total = half[0]
    for k, copy in enumerate(sends):
        copy.wait()
        total = total + land[k + 1]
    total = jnp.concatenate([total[j] for j in range(halves)], 1)
    inputs = matmul(total, gain[...])

    entering = carry[me]
    for k, copy in enumerate(carries):
        copy.wait()
        entering = entering + carry_land[k + 1]

    first = put_row(jnp.zeros_like(inputs), entering[0:1], 0)
    filtered = inputs + matmul(first, filt[0])
    for h in range(depth):
        filtered = filtered + matmul(shift(filtered, 1 << h), filt[h])
    filtered_ref[...] = filtered
    following = put_row(jnp.zeros_like(inputs), entering[1:2], length - 1)
    smoothed = filtered + matmul(following - filtered, back[0])
    for h in range(depth):
        smoothed = smoothed + matmul(shift(smoothed, -(1 << h)), back[h])
    smoothed_ref[...] = smoothed


def per_device(
    gauge_series, gauge_order, gauge_block, gauge_weight, filt_trans, obs_gain, smooth_gain
):
    devices = lax.axis_size("tm")
    steps, columns = gauge_series.shape
    states = filt_trans.shape[0]
    length = steps // devices
    chips = devices // 2
    depth = length.bit_length() - 1
    scans = devices.bit_length() - 1
    halves = states // LANES
    out = jax.ShapeDtypeStruct((length, states), jnp.float32)
    square = (states, states)
    return pl.pallas_call(
        functools.partial(kernel, devices),
        out_shape=(out, out),
        in_specs=[pl.BlockSpec(memory_space=pltpu.VMEM)] * 7,
        out_specs=[pl.BlockSpec(memory_space=pltpu.VMEM)] * 2,
        scratch_shapes=[
            pltpu.VMEM((halves, steps, LANES), jnp.float32),
            pltpu.VMEM((chips, halves, length, LANES), jnp.float32),
            pltpu.VMEM((chips, halves, length, LANES), jnp.float32),
            pltpu.VMEM((devices, 2, states), jnp.float32),
            pltpu.VMEM((devices, 2, states), jnp.float32),
            pltpu.VMEM((depth + scans,) + square, jnp.float32),
            pltpu.VMEM((depth + scans,) + square, jnp.float32),
            pltpu.VMEM((depth,) + square, jnp.float32),
            pltpu.VMEM(square, jnp.float32),
            pltpu.VMEM(square, jnp.float32),
            pltpu.VMEM((steps, states), jnp.float32),
            pltpu.VMEM((steps, states), jnp.float32),
            pltpu.VMEM((2, devices, states), jnp.float32),
            pltpu.SemaphoreType.DMA((chips,)),
            pltpu.SemaphoreType.DMA((chips,)),
            pltpu.SemaphoreType.DMA((chips,)),
            pltpu.SemaphoreType.DMA((chips,)),
            pltpu.SemaphoreType.DMA((devices,)),
            pltpu.SemaphoreType.DMA((devices,)),
        ],
        compiler_params=pltpu.CompilerParams(
            collective_id=0, has_side_effects=True, vmem_limit_bytes=56 << 20
        ),
    )(
        gauge_series,
        gauge_order.reshape(devices, 1, columns),
        gauge_block.reshape(1, -1),
        gauge_weight.T,
        filt_trans,
        obs_gain,
        smooth_gain,
    )


def solution(mesh):
    placed = (
        P("groups", "tm"),
        P(),
        P(),
        P(),
        P("groups", None),
        P("groups", None),
        P("groups", None),
    )
    return jax.shard_map(
        per_device,
        mesh=mesh,
        in_specs=placed,
        out_specs=(P(("groups", "tm"), None), P(("groups", "tm"), None)),
        check_vma=False,
    )
```

time: 130 us -> 38.5 us (0.30)
  local copies, waits for them, and re-layouts: 43.8 us -> 2.14 us
  matrix products: 40.4 us -> 0 us
  blocking collectives: 36.8 us -> 0 us
  Pallas kernels: 0 us -> 35.5 us
  other arithmetic: 6.51 us -> 0 us
  between operations: 2.07 us -> 0.65 us
    dot_general x59 -> x0, matrix products: 40.4 us -> none  [the longest x58 39.9 us: matmul(): jnp.dot(left, right, precision=PRECISE, preferred_element_type=jnp.float32)]
    all_to_all x1 -> x0, blocking collectives: 36.8 us -> none  [per_device(): lax.all_to_all(packed, 'tm', split_axis=0, concat_axis=0, tiled=True)]
    pallas_call x0 -> x1, Pallas kernels: none -> 35.5 us  [per_device(): pl.pallas_call(functools.partial(kernel, devices), out_shape=(out, out),...]
    reshape x12 -> x0, local copies, waits for them, and re-layouts: 12.6 us -> none  [the longest x6 6.92 us: per_device(): starts = starts.reshape(-1, 2, states)]
    unnamed x116 -> x4, local copies, waits for them, and re-layouts: 14.6 us -> 2.14 us
    slice x35 -> x0, local copies, waits for them, and re-layouts: 10.5 us -> none  [the longest x6 5.68 us: per_device(): starts[:, 1]]
    gather x3 -> x0, local copies, waits for them, and re-layouts: 4.58 us -> none  [the longest x1 3.14 us: per_device(): blocks = gauge_block.at[mine].get(mode='promise_in_bounds')]
    add x7 -> x0, other arithmetic: 1.73 us -> none  [the longest x6 1.7 us: per_device(): ends = ends[:, 1] + wide[:, :states]]
where the time goes in v2:
time: 38.5 us; the launch traced here: 38.3 us
  Pallas kernels  35.5 us (92%)
  local copies, waits for them, and re-layouts  2.14 us (6%)
  between operations  0.65 us (2%)
    pallas_call x1, Pallas kernels, per_device(): pl.pallas_call(functools.partial(kernel, devices), out_shape=(out, out),...  35.5 us
    unnamed x4, local copies, waits for them, and re-layouts  2.14 us

profile of v2, /device:TPU:0, one launch (start us, length us, event | category | flops | bytes accessed | tf_op | source)
XLA Modules:
  0.0 38.3 jit_solution(1367046067860078205)
XLA Ops:
  0.6 35.5 %shard_map.86 = (f32[64,256]{1,0:T(8,128)}, f32[64,256]{1,0:T(8,128)}) custom-call(bf16[1024,512]{1,0:T(8,128)(2,1)} %series_ref.1, s32[16,1,512]{2,1,0:T(1,128)} %bitcast.4, s32[1,8192]{1,0:T(1,128)} %bitcast.5, bf16[64,8192]{1,0:T(8,128)(2,1)} %bitcast.3, f32[256,256]{1,0:T(8,128)} %filt_in.1, f32[256,256]{1,0:T(8,128)} %gain_in.1, f32[256,256]{1,0:T(8,128)} %back_in.1), custom_call_target="tpu_custom_call" | custom-call | tf_op jit(solution)/shard_map/pallas_call | solution.py:263
  36.2 0.0 copy-start
  36.2 1.5 %copy.11 = f32[64,256]{1,0:T(8,128)} copy(f32[64,256]{1,0:T(8,128)} %get-tuple-element.4) | data formatting | bytes 131072
  37.7 0.0 copy-done
  37.7 0.6 %copy.12 = f32[64,256]{1,0:T(8,128)} copy(f32[64,256]{1,0:T(8,128)S(1)} %copy-done) | data formatting | bytes 131072
Async XLA Ops:
  36.2 1.5 %copy-start = (f32[64,256]{1,0:T(8,128)S(1)}, f32[64,256]{1,0:T(8,128)}, u32[]{:S(2)}) copy-start(f32[64,256]{1,0:T(8,128)} %get-tuple-element.5) | copy-start | bytes 196612

commit v3 on v2

--- a/solution.py
+++ b/solution.py
@@ -14,6 +14,19 @@
 
 def matmul(left, right):
     return jnp.dot(left, right, precision=PRECISE, preferred_element_type=jnp.float32)
+
+
+def split(values):
+    high = values.astype(jnp.bfloat16)
+    return high, (values - high.astype(jnp.float32)).astype(jnp.bfloat16)
+
+
+def matmul3(left, right):
+    high, low = split(left)
+    top, rest = split(right)
+    cross = jnp.dot(high, rest, preferred_element_type=jnp.float32)
+    cross = cross + jnp.dot(low, top, preferred_element_type=jnp.float32)
+    return cross + jnp.dot(high, top, preferred_element_type=jnp.float32)
 
 
 def shift(values, offset):
@@ -164,18 +177,18 @@
             sends.append(copy)
 
     for h in range(depth):
-        crossed[h] = matmul(enter[...], back[h])
+        crossed[h] = matmul3(enter[...], back[h])
         back[h + 1] = matmul(back[h], back[h])
         filt[h + 1] = matmul(filt[h], filt[h])
-        enter[...] = enter[...] + matmul(filt[h], crossed[h])
+        enter[...] = enter[...] + matmul3(filt[h], crossed[h])
     for h in range(depth, depth + scans - 1):
         filt[h + 1] = matmul(filt[h], filt[h])
         back[h + 1] = matmul(back[h], back[h])
 
     for base in range(0, steps, chunk):
         here = slice(base, base + chunk)
-        ends[here] = matmul(ends[here], gain[...])
-        starts[here] = ends[here] - matmul(ends[here], back[0])
+        ends[here] = matmul3(ends[here], gain[...])
+        starts[here] = ends[here] - matmul3(ends[here], back[0])
     rows = steps
     for h in range(depth):
         rows //= 2
@@ -185,9 +198,9 @@
             there = slice(rows + base, rows + base + part)
             left = ends[here]
             starts[here] = (
-                starts[here] + matmul(starts[there], back[h]) + matmul(left, crossed[h])
+                starts[here] + matmul3(starts[there], back[h]) + matmul3(left, crossed[h])
             )
-            ends[here] = ends[there] + matmul(left, filt[h])
+            ends[here] = ends[there] + matmul3(left, filt[h])
 
     for b in range(devices):
         source = (b % 2) * chips + b // 2
@@ -196,14 +209,14 @@
     reached = small[0]
     opened = small[1]
     for h in range(scans):
-        reached = reached + matmul(shift(reached, 1 << h), filt[depth + h])
+        reached = reached + matmul3(shift(reached, 1 << h), filt[depth + h])
     arrive = shift(reached, 1)
     final = reached[devices - 1 : devices]
-    opened = opened + matmul(arrive, enter[...])
+    opened = opened + matmul3(arrive, enter[...])
     leaving = put_row(jnp.zeros_like(opened), final, devices - 1)
-    opened = opened + matmul(leaving, back[depth])
+    opened = opened + matmul3(leaving, back[depth])
     for h in range(scans):
-        opened = opened + matmul(shift(opened, -(1 << h)), back[depth + h])
+        opened = opened + matmul3(shift(opened, -(1 << h)), back[depth + h])
     arrive_back = put_row(shift(opened, -1), final, devices - 1)
     for b in range(devices):
         carry[b, 0:1] = arrive[b : b + 1]
@@ -228,7 +241,7 @@
         copy.wait()
         total = total + land[k + 1]
     total = jnp.concatenate([total[j] for j in range(halves)], 1)
-    inputs = matmul(total, gain[...])
+    inputs = matmul3(total, gain[...])
 
     entering = carry[me]
     for k, copy in enumerate(carries):
@@ -236,14 +249,14 @@
         entering = entering + carry_land[k + 1]
 
     first = put_row(jnp.zeros_like(inputs), entering[0:1], 0)
-    filtered = inputs + matmul(first, filt[0])
+    filtered = inputs + matmul3(first, filt[0])
     for h in range(depth):
-        filtered = filtered + matmul(shift(filtered, 1 << h), filt[h])
+        filtered = filtered + matmul3(shift(filtered, 1 << h), filt[h])
     filtered_ref[...] = filtered
     following = put_row(jnp.zeros_like(inputs), entering[1:2], length - 1)
-    smoothed = filtered + matmul(following - filtered, back[0])
+    smoothed = filtered + matmul3(following - filtered, back[0])
     for h in range(depth):
-        smoothed = smoothed + matmul(shift(smoothed, -(1 << h)), back[h])
+        smoothed = smoothed + matmul3(shift(smoothed, -(1 << h)), back[h])
     smoothed_ref[...] = smoothed
 
 

time: 38.5 us -> 30.6 us (0.79)
  Pallas kernels: 35.5 us -> 27.6 us
    pallas_call x1, Pallas kernels: 35.5 us -> 27.6 us  [per_device(): pl.pallas_call(functools.partial(kernel, devices), out_shape=(out, out),...]
where the time goes in v3:
time: 30.6 us; the launch traced here: 30.4 us
  Pallas kernels  27.6 us (90%)
  local copies, waits for them, and re-layouts  2.14 us (7%)
  between operations  0.65 us (2%)
    pallas_call x1, Pallas kernels, per_device(): pl.pallas_call(functools.partial(kernel, devices), out_shape=(out, out),...  27.6 us
    unnamed x4, local copies, waits for them, and re-layouts  2.14 us

profile of v3, /device:TPU:0, one launch (start us, length us, event | category | flops | bytes accessed | tf_op | source)
XLA Modules:
  0.0 30.4 jit_solution(6395672167277201196)
XLA Ops:
  0.6 27.6 %shard_map.86 = (f32[64,256]{1,0:T(8,128)}, f32[64,256]{1,0:T(8,128)}) custom-call(bf16[1024,512]{1,0:T(8,128)(2,1)} %series_ref.1, s32[16,1,512]{2,1,0:T(1,128)} %bitcast.4, s32[1,8192]{1,0:T(1,128)} %bitcast.5, bf16[64,8192]{1,0:T(8,128)(2,1)} %bitcast.3, f32[256,256]{1,0:T(8,128)} %filt_in.1, f32[256,256]{1,0:T(8,128)} %gain_in.1, f32[256,256]{1,0:T(8,128)} %back_in.1), custom_call_target="tpu_custom_call" | custom-call | tf_op jit(solution)/shard_map/pallas_call | solution.py:276
  28.2 0.0 copy-start
  28.2 1.5 %copy.11 = f32[64,256]{1,0:T(8,128)} copy(f32[64,256]{1,0:T(8,128)} %get-tuple-element.4) | data formatting | bytes 131072
  29.7 0.0 copy-done
  29.8 0.6 %copy.12 = f32[64,256]{1,0:T(8,128)} copy(f32[64,256]{1,0:T(8,128)S(1)} %copy-done) | data formatting | bytes 131072
Async XLA Ops:
  28.2 1.5 %copy-start = (f32[64,256]{1,0:T(8,128)S(1)}, f32[64,256]{1,0:T(8,128)}, u32[]{:S(2)}) copy-start(f32[64,256]{1,0:T(8,128)} %get-tuple-element.5) | copy-start | bytes 196612

commit v4 on v3

--- a/solution.py
+++ b/solution.py
@@ -101,8 +101,8 @@
     piece = min(1024, gauges)
     gathered = None
     for base in range(0, gauges, piece):
-        spot = lax.broadcasted_iota(jnp.int32, (piece, order.shape[1]), 0) + base
-        onehot = jnp.where(spot == order, 1.0, 0.0).astype(jnp.bfloat16)
+        spot = lax.broadcasted_iota(jnp.int32, (piece, order.shape[1]), 0)
+        onehot = jnp.where(spot == order - base, 1.0, 0.0).astype(jnp.bfloat16)
         blocks = block_ref[:, base : base + piece].astype(jnp.float32)
         blocks = jnp.broadcast_to(blocks, (16, piece)).astype(jnp.bfloat16)
         table = jnp.concatenate([weight_ref[:, base : base + piece], blocks], 0)
@@ -156,7 +156,6 @@
     gain[...] = gain_in[...].T
     filt[0] = filt_in[...].T
     back[0] = back_in[...].T
-    enter[...] = filt[0] - matmul(filt[0], back[0])
 
     sends = []
     for k in range(chips):
@@ -176,6 +175,7 @@
             copy.start()
             sends.append(copy)
 
+    enter[...] = filt[0] - matmul(filt[0], back[0])
     for h in range(depth):
         crossed[h] = matmul3(enter[...], back[h])
         back[h + 1] = matmul(back[h], back[h])

time: 30.6 us -> 31 us (1.013)
  Pallas kernels: 27.6 us -> 28 us
    pallas_call x1, Pallas kernels: 27.6 us -> 28 us  [per_device(): pl.pallas_call(functools.partial(kernel, devices), out_shape=(out, out),...]
where the time goes in v4:
time: 31 us; the launch traced here: 30.8 us
  Pallas kernels  28 us (90%)
  local copies, waits for them, and re-layouts  2.14 us (7%)
  between operations  0.65 us (2%)
    pallas_call x1, Pallas kernels, per_device(): pl.pallas_call(functools.partial(kernel, devices), out_shape=(out, out),...  28 us
    unnamed x4, local copies, waits for them, and re-layouts  2.14 us

profile of v4, /device:TPU:0, one launch (start us, length us, event | category | flops | bytes accessed | tf_op | source)
XLA Modules:
  0.0 30.8 jit_solution(1814673576878285574)
XLA Ops:
  0.6 28.0 %shard_map.86 = (f32[64,256]{1,0:T(8,128)}, f32[64,256]{1,0:T(8,128)}) custom-call(bf16[1024,512]{1,0:T(8,128)(2,1)} %series_ref.1, s32[16,1,512]{2,1,0:T(1,128)} %bitcast.4, s32[1,8192]{1,0:T(1,128)} %bitcast.5, bf16[64,8192]{1,0:T(8,128)(2,1)} %bitcast.3, f32[256,256]{1,0:T(8,128)} %filt_in.1, f32[256,256]{1,0:T(8,128)} %gain_in.1, f32[256,256]{1,0:T(8,128)} %back_in.1), custom_call_target="tpu_custom_call" | custom-call | tf_op jit(solution)/shard_map/pallas_call | solution.py:276
  28.7 0.0 copy-start
  28.7 1.5 %copy.11 = f32[64,256]{1,0:T(8,128)} copy(f32[64,256]{1,0:T(8,128)} %get-tuple-element.4) | data formatting | bytes 131072
  30.2 0.0 copy-done
  30.2 0.6 %copy.12 = f32[64,256]{1,0:T(8,128)} copy(f32[64,256]{1,0:T(8,128)S(1)} %copy-done) | data formatting | bytes 131072
Async XLA Ops:
  28.7 1.5 %copy-start = (f32[64,256]{1,0:T(8,128)S(1)}, f32[64,256]{1,0:T(8,128)}, u32[]{:S(2)}) copy-start(f32[64,256]{1,0:T(8,128)} %get-tuple-element.5) | copy-start | bytes 196612
